TPU v7x, 512 devices: a whole 4x8x8 slice. The times are simulated.
512 devices in a mesh: col: 128 (over y, z, core), row: 4 (over x).
Axes of the slice: x: 4, y: 8, z: 8, core: 2. Of those that a mesh axis runs over, the one named last changes fastest.
Arguments:
- factor: float32 [128, 512, 1024], P('col', 'row'), may hold values from -0.6 to 0.6
- pattern: int32 [128, 4, 8], replicated, may hold values from 0 to 1, as said below
- order: int32 [128], replicated, may hold values from 0 to 127, each once
- targets: int32 [2, 2], replicated, may hold values from 0 to 3, as said below
- panels: float32 [512, 512], P('row'), may hold values from -6 to 6
Outputs:
- carried: float32 [128, 512, 512], P('col', 'row')
Inputs may be any that keep to these rules, and one draw needn't show every extreme that they name: `pattern`: 0 or 1 for each block of a supernode's rows and factored columns; the share of present blocks differs between supernodes. `targets`: every row block 0..3 is named at least once.
All inputs are finite; a program needn't handle non-finite values.
Results may differ from a plain program's by a relative error of at most 0.0001.
Values sent between devices are 32-bit elements; how exact they have to be, the bound alone decides.
A program may use at most 128 MiB of HBM per device.

v0:
```python
import jax
import jax.numpy as jnp
from jax import lax
from jax.sharding import Mesh
from jax.sharding import PartitionSpec as P

BLOCK = 128
COL = ("col_0", "col_1", "col_2")


def in_order(parts, dim):
    dims = list(parts.shape[1:])
    dims[dim] *= parts.shape[0]
    return jnp.moveaxis(parts, 0, dim).reshape(dims)


def sent_to_all(value, axis):
    devices = lax.axis_size(axis)
    return lax.all_to_all(
        jnp.broadcast_to(value[None], (devices, *value.shape)), axis, 0, 0, tiled=True
    )


def gathered_copies(value, axis, dim):
    return in_order(sent_to_all(value, axis), dim)


def filled_with(value, identity):
    return jnp.zeros_like(value) + jnp.asarray(identity, value.dtype)


def carried_in(value, axes, combine, identity):
    before = start = filled_with(value, identity)
    total = value
    for axis in reversed(axes):
        devices, place = (lax.axis_size(axis), lax.axis_index(axis))
        pieces = lax.all_gather(total, axis)
        inside, total = (start, start)
        for k in range(devices):
            passed = k < place
            total = combine(total, pieces[k])
            inside = jnp.where(passed, total, inside)
        before = combine(inside, before)
    return before


def product(masked, strips):
    return lax.dot_general(
        masked,
        strips,
        (((1,), (1,)), ((), ())),
        precision=lax.Precision.HIGHEST,
        preferred_element_type=jnp.float32,
    )


def combine(earlier, later):
    return earlier + later


def body(factor, pattern, order, targets, panels):
    owner_rows = factor[0]
    local_count = owner_rows.shape[0]
    width = owner_rows.shape[1]
    position = lax.axis_index(COL)
    row_place = lax.axis_index("row")
    chain_length = order.shape[0]
    supernode = jnp.sum(jnp.where(jnp.arange(chain_length, dtype=jnp.int32) == position, order, 0))
    picked = (jnp.arange(pattern.shape[0], dtype=jnp.int32) == supernode).astype(jnp.int32)
    owner_pattern = jnp.sum(picked[:, None, None] * pattern, axis=0)
    local_blocks = local_count // BLOCK
    col_blocks = width // BLOCK
    local_pattern = lax.dynamic_slice_in_dim(
        owner_pattern, row_place * local_blocks, local_blocks, 0
    )
    present = local_pattern.astype(jnp.float32)
    masked = (
        owner_rows.reshape(local_blocks, BLOCK, col_blocks, BLOCK) * present[:, None, :, None]
    ).reshape(local_count, width)
    gathered = gathered_copies(masked, "row", 0)
    strips = jnp.take(gathered.reshape(-1, BLOCK, width), targets.reshape(-1), axis=0).reshape(
        -1, width
    )
    update = product(masked, strips)
    empty = jnp.zeros_like(update)
    prior = carried_in(update, COL, combine, empty)
    carried = panels - prior - update
    return carried[None]


def solution(mesh):
    torus = Mesh(
        mesh.devices.reshape(8, 8, 2, mesh.shape["row"]), ("col_0", "col_1", "col_2", "row")
    )
    in_specs = (P(COL, "row", None), P(), P(), P(), P("row", None))
    out_specs = P(COL, "row", None)
    return jax.shard_map(body, mesh=torus, in_specs=in_specs, out_specs=out_specs, check_vma=False)
```

profile of v0, /device:TPU:4, one launch (start us, length us, event | category | flops | bytes accessed | tf_op | source)
XLA Modules:
  0.0 153.7 jit_solution(4818789033439763081)
XLA Ops:
  6.5 1.3 fusion.11
  7.8 0.6 compare_convert_fusion
  8.5 0.9 multiply_reduce_fusion
  9.4 0.1 broadcast_bitcast_fusion
  9.4 1.1 multiply_bitcast_fusion
  10.5 1.6 %broadcast_in_dim.29 = f32[4,128,1024]{2,1,0:T(8,128)} broadcast(f32[128,1024]{1,0:T(8,128)S(1)} %multiply_bitcast_fusion), dimensions={1,2} | broadcast | bytes 2621440 | tf_op jit(solution)/shard_map/broadcast_in_dim | solution.py:20
  12.2 0.0 copy-start.2
  12.2 9.6 %all-to-all-start = ((f32[4,128,1024]{2,1,0:T(8,128)}), f32[4,128,1024]{2,1,0:T(8,128)S(1)}, u32[]{:S(2)}, u32[]{:S(2)}) async-start(f32[4,128,1024]{2,1,0:T(8,128)} %broadcast_in_dim.29), calls=%async_computation | async-start | bytes 4194304 | tf_op jit(solution)/shard_map/all_to_all | solution.py:19
  21.7 0.0 all-gather.7.cloned.1.call-start
  21.8 0.0 copy-done.2
  21.8 0.1 reshape.127
  21.8 0.1 reshape.126
  21.9 18.5 %all-to-all-done = f32[4,128,1024]{2,1,0:T(8,128)S(1)} async-done(((f32[4,128,1024]{2,1,0:T(8,128)}), f32[4,128,1024]{2,1,0:T(8,128)S(1)}, u32[]{:S(2)}, u32[]{:S(2)}) %all-to-all-start) | async-done | bytes 2097184 | tf_op jit(solution)/shard_map/all_to_all | solution.py:19
  40.5 2.0 %gather_fusion = f32[4,128,1024]{2,1,0:T(8,128)} fusion(f32[4,128,1024]{2,1,0:T(8,128)S(1)} %all-to-all-done, s32[1024]{0:T(1024)S(1)} %pad_clamp_fusion), kind=kCustom, calls=%fused_computation | custom fusion | bytes 4194320 | tf_op jit(solution)/shard_map/jit(_take)/gather | solution.py:81
  42.5 1.9 %broadcast_select_fusion = f32[4,128,1024]{2,1,0:T(8,128)S(1)} fusion(f32[4,128,1024]{2,1,0:T(8,128)} %gather_fusion, pred[4]{0:T(512)(128)(4,1)S(1)} %compare_and_fusion), kind=kLoop, calls=%fused_computation.1 | loop fusion | flops 524288 | bytes 4194308 | tf_op jit(solution)/shard_map/jit(_take)/select_n | solution.py:81
  44.4 2.3 %fusion.13 = f32[128,512]{1,0:T(8,128)S(1)} fusion(f32[128,1024]{1,0:T(8,128)S(1)} %multiply_bitcast_fusion, f32[512,1024]{1,0:T(8,128)S(1)} %bitcast.55), kind=kOutput, calls=%fused_computation.42 | convolution fusion | flops 805306368 | bytes 2883584 | tf_op jit(solution)/shard_map/dot_general | solution.py:48
  46.6 2.2 %all-gather = f32[256,512]{1,0:T(8,128)S(1)} all-gather(f32[128,512]{1,0:T(8,128)S(1)} %fusion.13), channel_id=2, replica_groups=mesh['col_0'=8,'col_1'=8,'col_2'=2,'row'=4] {'col_2'}, dimensions={0}, use_global_device_ids=true | all-gather | bytes 786432 | tf_op jit(solution)/shard_map/all_gather | solution.py:37
  48.8 0.0 copy-start.1
  48.8 0.7 slice_add_fusion.12
  49.6 0.0 all-gather.7.cloned.1.call-update
  49.6 0.0 all-gather.5.cloned.1.call-start
  49.6 50.0 %all-gather.7.cloned.1.call-done = f32[1024,512]{1,0:T(8,128)} async-done(((f32[128,512]{1,0:T(8,128)}), f32[1024,512]{1,0:T(8,128)}) %all-gather.7.cloned.1.call-update) | async-done | bytes 2097168 | tf_op jit(solution)/shard_map/all_gather | solution.py:37
  99.6 0.0 copy-start
  99.6 2.6 %fusion.6 = (f32[1,128,512]{2,1,0:T(8,128)}, f32[128,512]{1,0:T(8,128)S(1)}) fusion(f32[1024,512]{1,0:T(8,128)} %all-gather.7.cloned.1.call-done), kind=kLoop, calls=%fused_computation.17 | loop fusion | flops 458752 | bytes 2621440 | tf_op jit(solution)/shard_map/add | solution.py:58
  102.2 0.0 all-gather.5.cloned.1.call-update
  102.2 41.7 %all-gather.5.cloned.1.call-done = f32[8,128,512]{2,1,0:T(8,128)} async-done(((f32[1,128,512]{2,1,0:T(8,128)}), f32[8,128,512]{2,1,0:T(8,128)}) %all-gather.5.cloned.1.call-update) | async-done | bytes 2097168 | tf_op jit(solution)/shard_map/all_gather | solution.py:37
  144.0 0.0 copy-done.1
  144.0 0.0 copy-done
  144.0 2.9 %fusion.5 = f32[1,128,512]{2,1,0:T(8,128)} fusion(f32[128,512]{1,0:T(8,128)S(1)} %fusion.13, f32[128,512]{1,0:T(8,128)S(1)} %copy-done.1, f32[8,128,512]{2,1,0:T(8,128)} %all-gather.5.cloned.1.call-done, f32[1,128,512]{2,1,0:T(8,128)} %get-tuple-element.5, f32[128,512]{1,0:T(8,128)S(1)} %get-tuple-element.6, f32[1024,512]{1,0:T(8,128)S(1)} %copy-done, ...), kind=kLoop, calls=%fused_computation.9 | loop fusion | flops 2293760 | bytes 5505042 | tf_op jit(solution)/shard_map/broadcast_in_dim | solution.py:88
  (4 shorter events, 0.0 us)
Async XLA Ops:
  12.2 9.6 %copy-start.2 = (s32[2,2]{1,0:T(2,128)S(1)}, s32[2,2]{1,0:T(2,128)}, u32[]{:S(2)}) copy-start(s32[2,2]{1,0:T(2,128)} %param.8) | copy-start | bytes 52
  12.2 28.3 %all-to-all-start = ((f32[4,128,1024]{2,1,0:T(8,128)}), f32[4,128,1024]{2,1,0:T(8,128)S(1)}, u32[]{:S(2)}, u32[]{:S(2)}) async-start(f32[4,128,1024]{2,1,0:T(8,128)} %broadcast_in_dim.29), calls=%async_computation | async-start | bytes 4194304 | tf_op jit(solution)/shard_map/all_to_all | solution.py:19
  21.7 77.9 %all-gather.7.cloned.1.call-start = ((), (), s32[]{:S(2)}) async-start(), calls=%async_computation.2 | async-start | bytes 2359296 | tf_op jit(solution)/shard_map/all_gather | solution.py:37
  48.8 95.1 %copy-start.1 = (f32[128,512]{1,0:T(8,128)S(1)}, f32[128,512]{1,0:T(8,128)}, u32[]{:S(2)}) copy-start(f32[128,512]{1,0:T(8,128)} %param.9) | copy-start | bytes 786436
  49.6 94.4 %all-gather.5.cloned.1.call-start = ((), (), s32[]{:S(2)}) async-start(), calls=%async_computation.1 | async-start | bytes 2359296 | tf_op jit(solution)/shard_map/all_gather | solution.py:37
  99.6 44.4 %copy-start = (f32[1024,512]{1,0:T(8,128)S(1)}, f32[1024,512]{1,0:T(8,128)}, u32[]{:S(2)}) copy-start(f32[1024,512]{1,0:T(8,128)} %all-gather.7.cloned.1.call-done) | copy-start | bytes 6291460
Sparse Core Ops, SparseCore 0:
  49.7 49.8 all-gather.6
  102.3 41.5 all-gather.4
where the time goes:
time: 154 us
  waiting for transfers between devices  110 us (71%)
  between operations  13.5 us (9%)
  other arithmetic  12 us (8%)
  starting transfers between devices  9.63 us (6%)
  local copies, waits for them, and re-layouts  3.91 us (3%)
  matrix products  2.26 us (1%)
  blocking collectives  2.18 us (1%)
    all_gather x2, waiting for transfers between devices, carried_in(): pieces = lax.all_gather(total, axis)  91.7 us
    all_to_all x1, waiting for transfers between devices, sent_to_all(): lax.all_to_all(jnp.broadcast_to(value[None], (devices, *value.shape)), ax...  18.5 us
    all_to_all x1, starting transfers between devices, sent_to_all(): lax.all_to_all(jnp.broadcast_to(value[None], (devices, *value.shape)), ax...  9.59 us
    add x2, other arithmetic, combine(): return earlier + later  3.3 us
  transfers between devices with their start and end apart: 3, of which 3 were waited for; matrix products, arithmetic and copies ran while one was open for 0% of the time, Pallas kernels for 0%

commit v1 on v0

v1 whole, which is shorter than its diff:
```python
import jax
import jax.numpy as jnp
from jax import lax
from jax.experimental import pallas as pl
from jax.experimental.pallas import tpu as pltpu
from jax.sharding import Mesh
from jax.sharding import PartitionSpec as P

BLOCK = 128
TILE = 8
NX, NY, NZ, NC = 4, 8, 8, 2
NQ = NZ * NC
MESH = pl.DeviceIdType.MESH
COL = ("y", "z", "core")
OWN, NEAR, FAR = 0, 1, 2


def split(value):
    high = value.astype(jnp.bfloat16)
    return high, (value - high.astype(jnp.float32)).astype(jnp.bfloat16)


def product(ah, al, bh, bl):
    def dot(a, b):
        return lax.dot_general(
            a, b, (((1,), (1,)), ((), ())), preferred_element_type=jnp.float32
        )

    return dot(ah, bh) + (dot(ah, bl) + dot(al, bh))


def kernel(
    order_ref, targets_ref, pattern_ref, factor_ref, panels_ref, out_ref,
    own, near, far, high, low, fhigh, flow, mask, pan,
    u, f, tot, yb, e, ret, rt,
    heavy_send, heavy_recv, local_sem,
    fwd_send, fwd_recv, y_send, y_recv, ret_send, ret_recv, rt_send, rt_recv,
):
    x, y, z, c = (lax.axis_index(a) for a in ("x", "y", "z", "core"))
    q = z * NC + c
    position = y * NQ + q
    ahead = lax.rem(x + 1 + 2 * c, NX)
    behind = lax.rem(x + 3 + 2 * c, NX)
    up, down, across = lax.rem(x + 1, NX), lax.rem(x + 3, NX), lax.rem(x + 2, NX)

    def at(x_, y_, q_):
        return (y_, q_ // NC, lax.rem(q_, NC), x_)

    def half(row):
        return pl.ds(pl.multiple_of((row // 2) * 512, 512), 512)

    def other(row):
        return pl.ds(pl.multiple_of((1 - row // 2) * 512, 512), 512)

    load_own = pltpu.make_async_copy(factor_ref.at[0], own, local_sem.at[0])
    load_pan = pltpu.make_async_copy(panels_ref, pan, local_sem.at[1])
    load_own.start()
    load_pan.start()

    with jax.named_scope("barrier"):
        barrier = pltpu.get_barrier_semaphore()
        for k in range(1, NX):
            pl.semaphore_signal(barrier, inc=1, device_id=at(lax.rem(x + k, NX), y, q), device_id_type=MESH)
        for k in range(1, NQ):
            pl.semaphore_signal(barrier, inc=1, device_id=at(x, y, lax.rem(q + k, NQ)), device_id_type=MESH)
        for k in range(1, NY):
            pl.semaphore_signal(barrier, inc=1, device_id=at(x, lax.rem(y + k, NY), q), device_id_type=MESH)
        pl.semaphore_wait(barrier, NX + NQ + NY - 3)

    def heavy(src, dst, i):
        return pltpu.make_async_remote_copy(
            src_ref=src, dst_ref=dst, send_sem=heavy_send.at[i], recv_sem=heavy_recv.at[i],
            device_id=at(ahead, y, q), device_id_type=MESH,
        )

    first = heavy(factor_ref.at[0, :, half(x)], near.at[:, half(x)], 0)
    second = heavy(factor_ref.at[0, :, other(x)], near.at[:, other(x)], 1)
    relay = heavy(near.at[:, half(behind)], far, 2)
    first.start()
    second.start()

    lanes = lax.broadcasted_iota(jnp.int32, (8, BLOCK), 1)
    picked = lanes == order_ref[position]
    for j in range(NX):
        kept = jnp.where(picked, pattern_ref[j], 0).astype(jnp.float32)
        mask[j] = jnp.broadcast_to(jnp.sum(kept, axis=1, keepdims=True), (8, BLOCK))

    def prepare(src, row, first_block, blocks, put):
        for k in range(blocks):
            columns = pl.ds(k * BLOCK, BLOCK)
            masked = src[:, columns] * mask[row, pl.ds(first_block + k, 1), :]
            put(columns, *split(masked))

    def put_at(slot):
        def put(columns, h, l):
            high[slot, :, columns] = h
            low[slot, :, columns] = l

        return put

    def put_far(columns, h, l):
        fhigh[:, columns] = h
        flow[:, columns] = l

    def keep(g, value):
        u[g] = value.reshape(NQ, TILE, BLOCK)

    def send_tiles(src, dst, send, recv, row, start):
        for k in range(start, NQ):
            peer = lax.rem(q + k, NQ)
            pltpu.make_async_remote_copy(
                src_ref=src.at[peer], dst_ref=dst.at[q], send_sem=send, recv_sem=recv,
                device_id=at(row, y, peer), device_id_type=MESH,
            ).start()

    def wait_tiles(buffer, count, sem):
        part = buffer.at[pl.ds(0, count)]
        pltpu.make_async_copy(part, part, sem).wait()

    def forward(g):
        send_tiles(u.at[g], f.at[g], fwd_send.at[g], fwd_recv.at[g], x, 1)
        f[g, q] = u[g, q]

    def scan(g):
        total = f[g, 0]
        e[g, 0] = total
        for s in range(1, NQ):
            total = total + f[g, s]
            e[g, s] = total
        tot[g] = total
        for k in range(1, NY):
            peer = lax.rem(y + k, NY)
            pltpu.make_async_remote_copy(
                src_ref=tot.at[g], dst_ref=yb.at[g, y], send_sem=y_send.at[g], recv_sem=y_recv.at[g],
                device_id=at(x, peer, q), device_id_type=MESH,
            ).start()

    def give_back(g):
        wait_tiles(yb.at[g], NY - 1, y_recv.at[g])
        before = jnp.zeros((TILE, BLOCK), jnp.float32)
        for k in range(NY):
            before = before + jnp.where(k < y, yb[g, k], 0.0)
        for s in range(NQ):
            e[g, s] = e[g, s] + before
        send_tiles(e.at[g], ret.at[g], ret_send.at[g], ret_recv.at[g], x, 1)
        ret[g, q] = e[g, q]

    load_own.wait()
    with jax.named_scope("own"):
        prepare(own, x, 0, 8, put_at(c))
        keep(OWN, product(high[c], low[c], high[c], low[c]))
        forward(OWN)
    with jax.named_scope("relay_start"):
        first.wait_recv()
        relay.start()
    with jax.named_scope("own_scan"):
        wait_tiles(f.at[OWN], NQ - 1, fwd_recv.at[OWN])
        scan(OWN)
    with jax.named_scope("own_back"):
        give_back(OWN)

    with jax.named_scope("near_wait"):
        second.wait_recv()
    with jax.named_scope("near"):
        prepare(near, behind, 0, 8, put_at(1 - c))
        keep(NEAR, product(high[0], low[0], high[1], low[1]))

        @pl.when(c == 0)
        def _():
            forward(NEAR)

        @pl.when(c == 1)
        def _():
            send_tiles(u.at[NEAR], f.at[NEAR], fwd_send.at[NEAR], fwd_recv.at[NEAR], up, 0)

    with jax.named_scope("far_wait"):
        relay.wait_recv()
    with jax.named_scope("far"):
        prepare(far, across, (across // 2) * 4, 4, put_far)
        keep(FAR, product(high[c, :, half(across)], low[c, :, half(across)], fhigh[...], flow[...]))
        forward(FAR)

    with jax.named_scope("near_scan"):
        @pl.when(c == 0)
        def _():
            wait_tiles(f.at[NEAR], NQ - 1, fwd_recv.at[NEAR])

        @pl.when(c == 1)
        def _():
            wait_tiles(f.at[NEAR], NQ, fwd_recv.at[NEAR])

        scan(NEAR)
    with jax.named_scope("far_scan"):
        wait_tiles(f.at[FAR], NQ - 1, fwd_recv.at[FAR])
        scan(FAR)
    with jax.named_scope("near_back"):
        give_back(NEAR)
        send_tiles(e.at[NEAR], rt.at[0], rt_send.at[0], rt_recv.at[0], down, 0)
    with jax.named_scope("far_back"):
        give_back(FAR)
        send_tiles(e.at[FAR], rt.at[1], rt_send.at[1], rt_recv.at[1], across, 0)

    with jax.named_scope("ret_wait"):
        load_pan.wait()
        for g in (OWN, NEAR, FAR):
            wait_tiles(ret.at[g], NQ - 1, ret_recv.at[g])
        for g in range(2):
            wait_tiles(rt.at[g], NQ, rt_recv.at[g])
    with jax.named_scope("final"):
        square = (BLOCK, BLOCK)
        ret[3] = rt[0].reshape(square).T.reshape(NQ, TILE, BLOCK)
        ret[FAR] = ret[FAR] + rt[1].reshape(square).T.reshape(NQ, TILE, BLOCK)
        for s in range(4):
            rows = targets_ref[s // 2, s % 2]
            away = lax.rem(x - rows + NX, NX)
            columns = pl.ds(s * BLOCK, BLOCK)
            out_ref[0, :, columns] = pan[:, columns] - ret[away].reshape(square)

    with jax.named_scope("drain"):
        first.wait_send()
        second.wait_send()
        relay.wait_send()
        wait_tiles(u.at[OWN], NQ - 1, fwd_send.at[OWN])

        @pl.when(c == 0)
        def _():
            wait_tiles(u.at[NEAR], NQ - 1, fwd_send.at[NEAR])

        @pl.when(c == 1)
        def _():
            wait_tiles(u.at[NEAR], NQ, fwd_send.at[NEAR])

        wait_tiles(u.at[FAR], NQ - 1, fwd_send.at[FAR])
        for g in (OWN, NEAR, FAR):
            wait_tiles(yb.at[g], NY - 1, y_send.at[g])
            wait_tiles(e.at[g], NQ - 1, ret_send.at[g])
        for g in range(2):
            wait_tiles(e.at[g + 1], NQ, rt_send.at[g])


def body(factor, pattern, order, targets, panels):
    vm, sem = pltpu.VMEM, pltpu.SemaphoreType.DMA
    f32, bf16 = jnp.float32, jnp.bfloat16
    rows, width = factor.shape[1:]
    tiles = (NQ, TILE, BLOCK)
    return pl.pallas_call(
        kernel,
        out_shape=jax.ShapeDtypeStruct((1, *panels.shape), f32),
        in_specs=[
            pl.BlockSpec(memory_space=pltpu.SMEM),
            pl.BlockSpec(memory_space=pltpu.SMEM),
            pl.BlockSpec(memory_space=pltpu.VMEM),
            pl.BlockSpec(memory_space=pl.ANY),
            pl.BlockSpec(memory_space=pl.ANY),
        ],
        out_specs=pl.BlockSpec(memory_space=pltpu.VMEM),
        scratch_shapes=[
            vm((rows, width), f32), vm((rows, width), f32), vm((rows, width // 2), f32),
            vm((2, rows, width), bf16), vm((2, rows, width), bf16),
            vm((rows, width // 2), bf16), vm((rows, width // 2), bf16),
            vm((NX, 8, BLOCK), f32), vm(panels.shape, f32),
            vm((3, *tiles), f32), vm((3, *tiles), f32), vm((3, TILE, BLOCK), f32),
            vm((3, NY, TILE, BLOCK), f32), vm((3, *tiles), f32), vm((4, *tiles), f32), vm((2, *tiles), f32),
            sem((3,)), sem((3,)), sem((2,)),
            sem((3,)), sem((3,)), sem((3,)), sem((3,)), sem((3,)), sem((3,)), sem((2,)), sem((2,)),
        ],
        compiler_params=pltpu.CompilerParams(
            collective_id=0, has_side_effects=True, vmem_limit_bytes=32 * 2**20
        ),
        name="fan_in",
    )(order, targets, jnp.transpose(pattern, (1, 2, 0)), factor, panels)


def solution(mesh):
    torus = Mesh(mesh.devices.reshape(NY, NZ, NC, NX), (*COL, "x"))
    in_specs = (P(COL, "x", None), P(), P(), P(), P("x", None))
    return jax.shard_map(
        body, mesh=torus, in_specs=in_specs, out_specs=P(COL, "x", None), check_vma=False
    )
```

time: 154 us -> 52.2 us (0.34)
  the two profiles are of different devices: /device:TPU:4 before, /device:TPU:1 now
where the time goes in v1:
time: 52.2 us; the launch traced here: 52 us
  Pallas kernels  47.9 us (92%)
  local copies, waits for them, and re-layouts  4.09 us (8%)
    pallas_call x1, Pallas kernels, body(): pl.pallas_call(kernel, out_shape=jax.ShapeDtypeStruct((1, *panels.shape),...  47.9 us
    unnamed x11, local copies, waits for them, and re-layouts  4.09 us

profile of v1, /device:TPU:1, one launch (start us, length us, event | category | flops | bytes accessed | tf_op | source)
XLA Modules:
  0.0 52.0 jit_solution(15013594960102111436)
XLA Ops:
  0.0 0.0 copy-start.3
  0.0 0.0 copy-start.4
  0.0 0.7 %copy-done.3 = s32[2,2]{1,0:T(2,128)S(1)} copy-done((s32[2,2]{1,0:T(2,128)S(1)}, s32[2,2]{1,0:T(2,128)}, u32[]{:S(2)}) %copy-start.3) | copy-done | bytes 40
  0.7 0.0 copy-done.4
  0.7 0.0 copy-start
  0.7 1.0 %copy-done = f32[1,128,1024]{2,1,0:T(8,128)S(1)} copy-done((f32[1,128,1024]{2,1,0:T(8,128)S(1)}, f32[1,128,1024]{2,1,0:T(8,128)}, u32[]{:S(2)}) %copy-start) | copy-done | bytes 524312
  1.7 0.0 copy-start.1
  1.7 0.9 %copy-done.1 = f32[128,512]{1,0:T(8,128)S(1)} copy-done((f32[128,512]{1,0:T(8,128)S(1)}, f32[128,512]{1,0:T(8,128)}, u32[]{:S(2)}) %copy-start.1) | copy-done | bytes 262168
  2.7 0.0 copy-start.2
  2.7 0.7 %copy-done.2 = s32[128,4,8]{0,2,1:T(8,128)S(1)} copy-done((s32[128,4,8]{0,2,1:T(8,128)S(1)}, s32[128,4,8]{0,2,1:T(8,128)}, u32[]{:S(2)}) %copy-start.2) | copy-done | bytes 16408
  3.4 47.9 %fan_in.1 = f32[1,128,512]{2,1,0:T(8,128)S(1)} custom-call(s32[128]{0:T(128)S(1)} %copy-done.4, s32[2,2]{1,0:T(2,128)S(1)} %copy-done.3, s32[4,8,128]{2,1,0:T(8,128)S(1)} %bitcast.1, f32[1,128,1024]{2,1,0:T(8,128)S(1)} %copy-done, f32[128,512]{1,0:T(8,128)S(1)} %copy-done.1), custom_call_target="tpu_custom_call" | custom-call | tf_op jit(solution)/shard_map/fan_in/pallas_call | solution.py:246
  51.3 0.7 %copy.7 = f32[1,128,512]{2,1,0:T(8,128)} copy(f32[1,128,512]{2,1,0:T(8,128)S(1)} %fan_in.1) | data formatting | bytes 524288
Async XLA Ops:
  0.0 0.7 %copy-start.3 = (s32[2,2]{1,0:T(2,128)S(1)}, s32[2,2]{1,0:T(2,128)}, u32[]{:S(2)}) copy-start(s32[2,2]{1,0:T(2,128)} %targets_ref.1) | copy-start | bytes 52
  0.0 0.7 %copy-start.4 = (s32[128]{0:T(128)S(1)}, s32[128]{0:T(128)}, u32[]{:S(2)}) copy-start(s32[128]{0:T(128)} %order_ref.1) | copy-start | bytes 1540
  0.7 1.0 %copy-start = (f32[1,128,1024]{2,1,0:T(8,128)S(1)}, f32[1,128,1024]{2,1,0:T(8,128)}, u32[]{:S(2)}) copy-start(f32[1,128,1024]{2,1,0:T(8,128)} %factor_ref.1) | copy-start | bytes 1572868
  1.7 0.9 %copy-start.1 = (f32[128,512]{1,0:T(8,128)S(1)}, f32[128,512]{1,0:T(8,128)}, u32[]{:S(2)}) copy-start(f32[128,512]{1,0:T(8,128)} %panels_ref.1) | copy-start | bytes 786436
  2.7 0.7 %copy-start.2 = (s32[128,4,8]{0,2,1:T(8,128)S(1)}, s32[128,4,8]{0,2,1:T(8,128)}, u32[]{:S(2)}) copy-start(s32[128,4,8]{0,2,1:T(8,128)} %param.6) | copy-start | bytes 49156

commit v2 on v1

v2 whole, which is shorter than its diff:
```python
import jax
import jax.numpy as jnp
from jax import lax
from jax.experimental import pallas as pl
from jax.experimental.pallas import tpu as pltpu
from jax.sharding import Mesh
from jax.sharding import PartitionSpec as P

BLOCK = 128
NX, NY, NZ, NC = 4, 8, 8, 2
NQ = NZ * NC
NR = 16
ROWS = BLOCK // NR
BASE = 0 if NR == NQ else NQ - NR // 2
MESH = pl.DeviceIdType.MESH
COL = ("y", "z", "core")
OWN, NEAR, FAR = 0, 1, 2


def split(value):
    high = value.astype(jnp.bfloat16)
    return high, (value - high.astype(jnp.float32)).astype(jnp.bfloat16)


def product(ah, al, bh, bl):
    def dot(a, b):
        return lax.dot_general(
            a, b, (((1,), (1,)), ((), ())), preferred_element_type=jnp.float32
        )

    return dot(ah, bh) + (dot(ah, bl) + dot(al, bh))


def kernel(
    order_hbm, targets_hbm, pattern_hbm, factor_hbm, panels_hbm, out_ref,
    order_ref, targets_ref, pattern_ref, own, near, far, high, low, fhigh, flow, mask, pan,
    u, f, tot, yb, e, ret, rt,
    heavy_send, heavy_recv, local_sem,
    fwd_send, fwd_recv, y_send, y_recv, ret_send, ret_recv, rt_send, rt_recv,
):
    x, y, z, c = (lax.axis_index(a) for a in ("x", "y", "z", "core"))
    q = z * NC + c
    slot = lax.rem(q + NQ - BASE, NQ)
    scans = slot < NR
    position = y * NQ + q
    up, down, across = (lax.rem(x + k, NX) for k in (1, 3, 2))
    ahead = lax.rem(x + 1 + 2 * c, NX)
    behind = lax.rem(x + 3 + 2 * c, NX)

    def at(x_, y_, q_):
        return (y_, q_ // NC, lax.rem(q_, NC), x_)

    def scanner(j):
        return lax.rem(j + BASE, NQ)

    def half(row):
        return pl.ds(pl.multiple_of((row // 2) * 512, 512), 512)

    def other(row):
        return pl.ds(pl.multiple_of((1 - row // 2) * 512, 512), 512)

    loads = [
        pltpu.make_async_copy(a, b, local_sem.at[i])
        for i, (a, b) in enumerate((
            (factor_hbm.at[0], own), (order_hbm, order_ref), (pattern_hbm, pattern_ref),
            (targets_hbm, targets_ref), (panels_hbm, pan),
        ))
    ]
    for load in loads:
        load.start()

    barrier = pltpu.get_barrier_semaphore()

    def greet(device):
        pl.semaphore_signal(barrier, inc=1, device_id=device, device_id_type=MESH)

    for k in range(1, NX):
        greet(at(lax.rem(x + k, NX), y, q))
    for k in range(1, NQ):
        greet(at(x, y, lax.rem(q + k, NQ)))
    for k in range(1, NY):
        greet(at(x, lax.rem(y + k, NY), q))

    @pl.when(scans)
    def _():
        for k in range(NZ):
            greet(at(down, y, k * NC + 1))

    pl.semaphore_wait(barrier, NX + NQ + NY - 3 + c * NR)

    def exchange(src, dst, i, row):
        return pltpu.make_async_remote_copy(
            src_ref=src, dst_ref=dst, send_sem=heavy_send.at[i], recv_sem=heavy_recv.at[i],
            device_id=at(row, y, q), device_id_type=MESH,
        )

    first = exchange(factor_hbm.at[0, :, half(ahead)], near.at[:, half(ahead)], 0, ahead)
    second = exchange(factor_hbm.at[0, :, other(ahead)], near.at[:, other(ahead)], 1, ahead)
    third = exchange(factor_hbm.at[0, :, half(behind)], far, 2, behind)
    first.start()
    third.start()
    second.start()

    loads[1].wait()
    loads[2].wait()
    lanes = lax.broadcasted_iota(jnp.int32, (8, BLOCK), 1)
    picked = lanes == order_ref[position]
    for j in range(NX):
        kept = jnp.where(picked, pattern_ref[j], 0).astype(jnp.float32)
        mask[j] = jnp.broadcast_to(jnp.sum(kept, axis=1, keepdims=True), (8, BLOCK))

    def prepare(src, row, first_block, blocks, put):
        for k in range(blocks):
            columns = pl.ds(k * BLOCK, BLOCK)
            masked = src[:, columns] * mask[row, pl.ds(first_block + k, 1), :]
            put(columns, *split(masked))

    def put_at(place):
        def put(columns, h, l):
            high[place, :, columns] = h
            low[place, :, columns] = l

        return put

    def keep(g, value):
        u[g] = value.reshape(NR, ROWS, BLOCK)

    def send(src, dst, send_sem, recv_sem, device):
        pltpu.make_async_remote_copy(
            src_ref=src, dst_ref=dst, send_sem=send_sem, recv_sem=recv_sem,
            device_id=device, device_id_type=MESH,
        ).start()

    def wait_slots(buffer, count, sem):
        part = buffer.at[pl.ds(0, count)]
        pltpu.make_async_copy(part, part, sem).wait()

    def either(condition, small, large, buffer, sem):
        @pl.when(condition)
        def _():
            wait_slots(buffer, small, sem)

        @pl.when(jnp.logical_not(condition))
        def _():
            wait_slots(buffer, large, sem)

    def forward(g, row):
        for j in range(NR):
            to = scanner(j)

            @pl.when(jnp.logical_or(row != x, to != q))
            def _():
                send(u.at[g, j], f.at[g, q], fwd_send.at[g], fwd_recv.at[g], at(row, y, to))

        @pl.when(jnp.logical_and(scans, row == x))
        def _():
            f[g, q] = u[g, slot]

    def scan(g):
        total = f[g, 0]
        e[g, 0] = total
        for s in range(1, NQ):
            total = total + f[g, s]
            e[g, s] = total
        tot[g] = total
        for k in range(1, NY):
            @pl.when(k > y)
            def _():
                send(tot.at[g], yb.at[g, y], y_send.at[g, k], y_recv.at[g, y], at(x, k, q))

    def total_waits(g, earlier):
        for k in range(NY):
            @pl.when(k < y if earlier else k > y)
            def _():
                sem = y_recv if earlier else y_send
                pltpu.make_async_copy(yb.at[g, k], yb.at[g, k], sem.at[g, k]).wait()

    def add_earlier(g):
        total_waits(g, True)
        before = jnp.zeros((ROWS, BLOCK), jnp.float32)
        for k in range(NY):
            before = before + jnp.where(k < y, yb[g, k], 0.0)
        for s in range(NQ):
            e[g, s] = e[g, s] + before

    loads[0].wait()
    prepare(own, x, 0, 8, put_at(c))
    keep(OWN, product(high[c], low[c], high[c], low[c]))
    forward(OWN, x)

    @pl.when(scans)
    def _():
        wait_slots(f.at[OWN], NQ - 1, fwd_recv.at[OWN])
        scan(OWN)

    first.wait_recv()
    third.wait_recv()
    for k in range(4):
        columns = pl.ds(k * BLOCK, BLOCK)
        block = (x // 2) * 4 + k
        from_near = near[:, pl.ds(pl.multiple_of(block * BLOCK, BLOCK), BLOCK)]
        for place, (value, row) in enumerate(((from_near, behind), (far[:, columns], ahead))):
            h, l = split(value * mask[row, pl.ds(block, 1), :])
            side = c if place == 0 else 1 - c
            fhigh[side, :, columns] = h
            flow[side, :, columns] = l
    keep(FAR, product(fhigh[0], flow[0], fhigh[1], flow[1]))
    forward(FAR, x)

    second.wait_recv()
    prepare(near, behind, 0, 8, put_at(1 - c))
    keep(NEAR, product(high[0], low[0], high[1], low[1]))
    forward(NEAR, lax.rem(x + c, NX))

    @pl.when(scans)
    def _():
        add_earlier(OWN)
        for p in range(NQ):
            @pl.when(p != q)
            def _():
                send(e.at[OWN, p], ret.at[0, slot], ret_send.at[0], ret_recv.at[0], at(x, y, p))

        ret[0, slot] = e[OWN, q]
        wait_slots(f.at[FAR], NQ - 1, fwd_recv.at[FAR])
        scan(FAR)
        either(c == 0, NQ - 1, NQ, f.at[NEAR], fwd_recv.at[NEAR])
        scan(NEAR)
        add_earlier(FAR)
        for p in range(NQ):
            send(e.at[FAR, p], ret.at[2, slot], rt_send.at[1], ret_recv.at[2], at(down, y, p))
            send(e.at[FAR, p], rt.at[1, slot], rt_send.at[2], rt_recv.at[1], at(up, y, p))
        add_earlier(NEAR)
        for p in range(NQ):
            @pl.when(p != q)
            def _():
                send(e.at[NEAR, p], ret.at[1, slot], ret_send.at[1], ret_recv.at[1], at(x, y, p))

            send(e.at[NEAR, p], rt.at[0, slot], rt_send.at[0], rt_recv.at[0], at(down, y, p))
        ret[1, slot] = e[NEAR, q]

    loads[3].wait()
    loads[4].wait()
    either(scans, NR - 1, NR, ret.at[0], ret_recv.at[0])
    wait_slots(ret.at[2], NR, ret_recv.at[2])
    wait_slots(rt.at[1], NR, rt_recv.at[1])
    either(scans, NR - 1, NR, ret.at[1], ret_recv.at[1])
    wait_slots(rt.at[0], NR, rt_recv.at[0])
    square = (BLOCK, BLOCK)
    slots = (NR, ROWS, BLOCK)
    ret[3] = rt[0].reshape(square).T.reshape(slots)
    ret[2] = ret[2] + rt[1].reshape(square).T.reshape(slots)
    for s in range(4):
        away = lax.rem(x - targets_ref[s // 2, s % 2] + NX, NX)
        columns = pl.ds(s * BLOCK, BLOCK)
        out_ref[0, :, columns] = pan[:, columns] - ret[away].reshape(square)

    first.wait_send()
    second.wait_send()
    third.wait_send()
    for g in (OWN, FAR):
        either(scans, NR - 1, NR, u.at[g], fwd_send.at[g])
    either(jnp.logical_and(scans, c == 0), NR - 1, NR, u.at[NEAR], fwd_send.at[NEAR])

    @pl.when(scans)
    def _():
        for g in (OWN, NEAR, FAR):
            total_waits(g, False)
        for g in (OWN, NEAR):
            wait_slots(e.at[g], NQ - 1, ret_send.at[g])
        wait_slots(e.at[NEAR], NQ, rt_send.at[0])
        wait_slots(e.at[FAR], NQ, rt_send.at[1])
        wait_slots(e.at[FAR], NQ, rt_send.at[2])


def body(factor, pattern, order, targets, panels):
    vm, sem = pltpu.VMEM, pltpu.SemaphoreType.DMA
    f32, bf16 = jnp.float32, jnp.bfloat16
    rows, width = factor.shape[1:]
    tile = (ROWS, BLOCK)
    return pl.pallas_call(
        kernel,
        out_shape=jax.ShapeDtypeStruct((1, *panels.shape), f32),
        in_specs=[pl.BlockSpec(memory_space=pl.ANY) for _ in range(5)],
        out_specs=pl.BlockSpec(memory_space=pltpu.VMEM),
        scratch_shapes=[
            pltpu.SMEM((128,), jnp.int32), pltpu.SMEM((2, 2), jnp.int32), vm((NX, 8, BLOCK), jnp.int32),
            vm((rows, width), f32), vm((rows, width), f32), vm((rows, width // 2), f32),
            vm((2, rows, width), bf16), vm((2, rows, width), bf16),
            vm((2, rows, width // 2), bf16), vm((2, rows, width // 2), bf16),
            vm((NX, 8, BLOCK), f32), vm(panels.shape, f32),
            vm((3, NR, *tile), f32), vm((3, NQ, *tile), f32), vm((3, *tile), f32),
            vm((3, NY, *tile), f32), vm((3, NQ, *tile), f32), vm((4, NR, *tile), f32), vm((2, NR, *tile), f32),
            sem((3,)), sem((3,)), sem((5,)),
            sem((3,)), sem((3,)), sem((3, NY)), sem((3, NY)), sem((2,)), sem((3,)), sem((3,)), sem((2,)),
        ],
        compiler_params=pltpu.CompilerParams(
            collective_id=0, has_side_effects=True, vmem_limit_bytes=60 * 2**20
        ),
        name="fan_in",
    )(order, targets, jnp.transpose(pattern, (1, 2, 0)), factor, panels)


def solution(mesh):
    torus = Mesh(mesh.devices.reshape(NY, NZ, NC, NX), (*COL, "x"))
    in_specs = (P(COL, "x", None), P(), P(), P(), P("x", None))
    return jax.shard_map(
        body, mesh=torus, in_specs=in_specs, out_specs=P(COL, "x", None), check_vma=False
    )
```

time: 52.2 us -> 42.6 us (0.82)
  Pallas kernels: 47.9 us -> 40.8 us
  local copies, waits for them, and re-layouts: 4.09 us -> 1.67 us
    pallas_call x1, Pallas kernels: 47.9 us -> 40.8 us  [body(): pl.pallas_call(kernel, out_shape=jax.ShapeDtypeStruct((1, *panels.shape),...]
    unnamed x11 -> x1, local copies, waits for them, and re-layouts: 4.09 us -> 1.67 us
where the time goes in v2:
time: 42.6 us; the launch traced here: 42.5 us
  Pallas kernels  40.8 us (96%)
  local copies, waits for them, and re-layouts  1.67 us (4%)
    pallas_call x1, Pallas kernels, body(): pl.pallas_call(kernel, out_shape=jax.ShapeDtypeStruct((1, *panels.shape),...  40.8 us
    unnamed x1, local copies, waits for them, and re-layouts  1.67 us

profile of v2, /device:TPU:1, one launch (start us, length us, event | category | flops | bytes accessed | tf_op | source)
XLA Modules:
  0.0 42.5 jit_solution(14157071305425676792)
XLA Ops:
  0.0 40.8 %fan_in.1 = f32[1,128,512]{2,1,0:T(8,128)} custom-call(s32[128]{0:T(128)} %order_hbm.1, s32[2,2]{1,0:T(2,128)} %targets_hbm.1, s32[4,8,128]{2,1,0:T(8,128)} %bitcast.1, f32[1,128,1024]{2,1,0:T(8,128)} %factor_hbm.1, f32[128,512]{1,0:T(8,128)} %panels_hbm.1), custom_call_target="tpu_custom_call" | custom-call | tf_op jit(solution)/shard_map/fan_in/pallas_call | solution.py:280
  40.8 1.7 %copy.7 = f32[1,128,512]{2,1,0:T(8,128)} copy(f32[1,128,512]{2,1,0:T(8,128)} %fan_in.1) | data formatting | bytes 524288

commit v3 on v2

v3 whole, which is shorter than its diff:
```python
import jax
import jax.numpy as jnp
from jax import lax
from jax.experimental import pallas as pl
from jax.experimental.pallas import tpu as pltpu
from jax.sharding import Mesh
from jax.sharding import PartitionSpec as P

BLOCK = 128
NX, NY, NZ, NC = 4, 8, 8, 2
NQ = NZ * NC
NR = 16
ROWS = BLOCK // NR
BASE = 0 if NR == NQ else NQ - NR // 2
MESH = pl.DeviceIdType.MESH
COL = ("y", "z", "core")
OWN, NEAR, FAR = 0, 1, 2
FARTHEST_FIRST = (6, 7, 8, 9, 4, 5, 10, 11, 2, 3, 12, 13, 0, 1, 14, 15)


def split(value):
    high = value.astype(jnp.bfloat16)
    return high, (value - high.astype(jnp.float32)).astype(jnp.bfloat16)


def product(ah, al, bh, bl):
    def dot(a, b):
        return lax.dot_general(
            a, b, (((1,), (1,)), ((), ())), preferred_element_type=jnp.float32
        )

    return dot(ah, bh) + (dot(ah, bl) + dot(al, bh))


def kernel(
    order_hbm, pattern_hbm, factor_hbm, ret,
    order_ref, pattern_ref, own, near, far, high, low, fhigh, flow, mask,
    u, f, g, tot, yb, e,
    heavy_send, heavy_recv, local_sem,
    fwd_send, fwd_recv, y_send, y_recv, ret_send, ret_recv, rt_send, rt_recv,
):
    x, y, z, c = (lax.axis_index(a) for a in ("x", "y", "z", "core"))
    q = z * NC + c
    slot = lax.rem(q + NQ - BASE, NQ)
    scans = slot < NR
    joins = lax.rem(z, 2) == x // 2
    position = y * NQ + q
    up, down, across = (lax.rem(x + k, NX) for k in (1, 3, 2))
    ahead = lax.rem(x + 1 + 2 * c, NX)
    behind = lax.rem(x + 3 + 2 * c, NX)

    def at(x_, y_, q_):
        return (y_, q_ // NC, lax.rem(q_, NC), x_)

    def scanner(j):
        return lax.rem(j + BASE, NQ)

    def half(row):
        return pl.ds(pl.multiple_of((row // 2) * 512, 512), 512)

    def other(row):
        return pl.ds(pl.multiple_of((1 - row // 2) * 512, 512), 512)

    loads = [
        pltpu.make_async_copy(a, b, local_sem.at[i])
        for i, (a, b) in enumerate((
            (factor_hbm.at[0], own), (order_hbm, order_ref), (pattern_hbm, pattern_ref),
        ))
    ]
    for load in loads:
        load.start()

    barrier = pltpu.get_barrier_semaphore()

    def greet(device):
        pl.semaphore_signal(barrier, inc=1, device_id=device, device_id_type=MESH)

    for k in range(1, NX):
        greet(at(lax.rem(x + k, NX), y, q))
    for k in range(1, NQ):
        greet(at(x, y, lax.rem(q + k, NQ)))
    for k in range(1, NY):
        greet(at(x, lax.rem(y + k, NY), q))

    @pl.when(scans)
    def _():
        for k in range(NZ):
            greet(at(down, y, k * NC + 1))

    pl.semaphore_wait(barrier, NX + NQ + NY - 3 + c * NR)

    def exchange(src, dst, i, row):
        return pltpu.make_async_remote_copy(
            src_ref=src, dst_ref=dst, send_sem=heavy_send.at[i], recv_sem=heavy_recv.at[i],
            device_id=at(row, y, q), device_id_type=MESH,
        )

    first = exchange(factor_hbm.at[0, :, half(ahead)], near.at[:, half(ahead)], 0, ahead)
    second = exchange(factor_hbm.at[0, :, other(ahead)], near.at[:, other(ahead)], 1, ahead)
    third = exchange(factor_hbm.at[0, :, half(behind)], far, 2, behind)
    first.start()
    third.start()
    second.start()

    loads[1].wait()
    loads[2].wait()
    lanes = lax.broadcasted_iota(jnp.int32, (8, BLOCK), 1)
    picked = lanes == order_ref[position]
    for j in range(NX):
        kept = jnp.where(picked, pattern_ref[j], 0).astype(jnp.float32)
        mask[j] = jnp.broadcast_to(jnp.sum(kept, axis=1, keepdims=True), (8, BLOCK))

    def prepare(src, row, first_block, blocks, put):
        for k in range(blocks):
            columns = pl.ds(pl.multiple_of((first_block + k) * BLOCK, BLOCK), BLOCK)
            masked = src[:, columns] * mask[row, pl.ds(first_block + k, 1), :]
            put(columns, *split(masked))

    def put_at(place):
        def put(columns, h, l):
            high[place, :, columns] = h
            low[place, :, columns] = l

        return put

    def keep(b, value):
        u[b] = value.reshape(NR, ROWS, BLOCK)

    def send(src, dst, send_sem, recv_sem, device):
        pltpu.make_async_remote_copy(
            src_ref=src, dst_ref=dst, send_sem=send_sem, recv_sem=recv_sem,
            device_id=device, device_id_type=MESH,
        ).start()

    def wait_slots(buffer, count, sem):
        part = buffer.at[pl.ds(0, count)]
        pltpu.make_async_copy(part, part, sem).wait()

    def either(condition, small, large, buffer, sem):
        @pl.when(condition)
        def _():
            wait_slots(buffer, small, sem)

        @pl.when(jnp.logical_not(condition))
        def _():
            wait_slots(buffer, large, sem)

    def forward(b, row):
        for j in FARTHEST_FIRST:
            to = scanner(j)

            @pl.when(jnp.logical_or(row != x, to != q))
            def _():
                send(u.at[b, j], f.at[b, q], fwd_send.at[b], fwd_recv.at[b], at(row, y, to))

        @pl.when(jnp.logical_and(scans, row == x))
        def _():
            f[b, q] = u[b, slot]

    def scan(b, part):
        total = part(0)
        e[b, 0] = total
        for s in range(1, NQ):
            total = total + part(s)
            e[b, s] = total
        tot[b] = total
        for k in range(1, NY):
            @pl.when(k > y)
            def _():
                send(tot.at[b], yb.at[b, y], y_send.at[b, k], y_recv.at[b, y], at(x, k, q))

    def total_waits(b, earlier):
        for k in range(NY):
            @pl.when(k < y if earlier else k > y)
            def _():
                sem = y_recv if earlier else y_send
                pltpu.make_async_copy(yb.at[b, k], yb.at[b, k], sem.at[b, k]).wait()

    def add_earlier(b):
        total_waits(b, True)
        before = jnp.zeros((ROWS, BLOCK), jnp.float32)
        for k in range(NY):
            before = before + jnp.where(k < y, yb[b, k], 0.0)
        for s in range(NQ):
            e[b, s] = e[b, s] + before

    loads[0].wait()
    prepare(own, x, 0, 8, put_at(c))
    keep(OWN, product(high[c], low[c], high[c], low[c]))
    forward(OWN, x)

    @pl.when(scans)
    def _():
        wait_slots(f.at[OWN], NQ - 1, fwd_recv.at[OWN])
        scan(OWN, lambda s: f[OWN, s])

    first.wait_recv()
    third.wait_recv()
    for k in range(4):
        columns = pl.ds(k * BLOCK, BLOCK)
        block = (x // 2) * 4 + k
        from_near = near[:, pl.ds(pl.multiple_of(block * BLOCK, BLOCK), BLOCK)]
        for value, row in ((from_near, behind), (far[:, columns], ahead)):
            h, l = split(value * mask[row, pl.ds(block, 1), :])
            fhigh[row // 2, :, columns] = h
            flow[row // 2, :, columns] = l
    keep(FAR, product(fhigh[0], flow[0], fhigh[1], flow[1]))
    for j in FARTHEST_FIRST:
        row = jnp.where(lax.rem(j // NC, 2) == x // 2, x, across)

        @pl.when(jnp.logical_or(row != x, j != q))
        def _():
            send(u.at[FAR, j], g.at[x // 2, q], fwd_send.at[FAR], fwd_recv.at[FAR], at(row, y, j))

    @pl.when(joins)
    def _():
        g[x // 2, q] = u[FAR, slot]

    prepare(near, behind, (x // 2) * 4, 4, put_at(1 - c))
    second.wait_recv()
    prepare(near, behind, (1 - x // 2) * 4, 4, put_at(1 - c))
    keep(NEAR, product(high[0], low[0], high[1], low[1]))
    forward(NEAR, lax.rem(x + c, NX))

    @pl.when(scans)
    def _():
        add_earlier(OWN)
        for p in range(NQ):
            @pl.when(p != q)
            def _():
                send(e.at[OWN, p], ret.at[0, slot], ret_send.at[0], ret_recv.at[0], at(x, y, p))

        keep_own = pltpu.make_async_copy(e.at[OWN, q], ret.at[0, slot], local_sem.at[3])
        keep_own.start()

        @pl.when(joins)
        def _():
            flat = g.reshape(2 * NQ, ROWS, BLOCK)
            wait_slots(flat, 2 * NQ - 1, fwd_recv.at[FAR])
            scan(FAR, lambda s: g[0, s] + g[1, s])

        either(c == 0, NQ - 1, NQ, f.at[NEAR], fwd_recv.at[NEAR])
        scan(NEAR, lambda s: f[NEAR, s])

        def far_back(places):
            for p in places:
                send(e.at[FAR, p], ret.at[2, slot], rt_send.at[1], ret_recv.at[2], at(down, y, p))
                send(e.at[FAR, p], ret.at[2, slot], rt_send.at[2], ret_recv.at[2], at(up, y, p))

        def near_back(places):
            for p in places:
                @pl.when(p != q)
                def _():
                    send(e.at[NEAR, p], ret.at[1, slot], ret_send.at[1], ret_recv.at[1], at(x, y, p))

                send(e.at[NEAR, p], ret.at[3, slot], rt_send.at[0], rt_recv.at[0], at(down, y, p))

        @pl.when(joins)
        def _():
            add_earlier(FAR)
            far_back(range(NQ // 2))

        add_earlier(NEAR)
        near_back(range(NQ // 2))

        @pl.when(joins)
        def _():
            far_back(range(NQ // 2, NQ))

        near_back(range(NQ // 2, NQ))
        keep_near = pltpu.make_async_copy(e.at[NEAR, q], ret.at[1, slot], local_sem.at[4])
        keep_near.start()
        keep_own.wait()
        keep_near.wait()

    either(scans, NR - 1, NR, ret.at[0], ret_recv.at[0])
    wait_slots(ret.at[2], NR, ret_recv.at[2])
    either(scans, NR - 1, NR, ret.at[1], ret_recv.at[1])
    wait_slots(ret.at[3], NR, rt_recv.at[0])

    first.wait_send()
    second.wait_send()
    third.wait_send()
    wait_slots(u.at[OWN], NR - 1, fwd_send.at[OWN])
    either(joins, NR - 1, NR, u.at[FAR], fwd_send.at[FAR])
    either(jnp.logical_and(scans, c == 0), NR - 1, NR, u.at[NEAR], fwd_send.at[NEAR])

    @pl.when(scans)
    def _():
        for b in (OWN, NEAR):
            total_waits(b, False)
        for b in (OWN, NEAR):
            wait_slots(e.at[b], NQ - 1, ret_send.at[b])
        wait_slots(e.at[NEAR], NQ, rt_send.at[0])

        @pl.when(joins)
        def _():
            total_waits(FAR, False)
            wait_slots(e.at[FAR], NQ, rt_send.at[1])
            wait_slots(e.at[FAR], NQ, rt_send.at[2])


def finish(targets_hbm, ret_hbm, panels_hbm, out_hbm, targets_ref, ret, pan, out, sems, out_sems):
    x = lax.axis_index("x")
    square = (BLOCK, BLOCK)
    loads = [pltpu.make_async_copy(ret_hbm.at[k], ret.at[k], sems.at[k]) for k in range(4)]
    loads.append(pltpu.make_async_copy(panels_hbm, pan, sems.at[4]))
    loads.append(pltpu.make_async_copy(targets_hbm, targets_ref, sems.at[5]))
    for load in loads:
        load.start()
    for load in loads:
        load.wait()
    ret[3] = ret[3].reshape(square).T.reshape(ret.shape[1:])
    pair = ret[2].reshape(square)
    ret[2] = jnp.where(x < 2, pair, pair.T).reshape(ret.shape[1:])
    stores = []
    for s in range(4):
        away = lax.rem(x - targets_ref[s // 2, s % 2] + NX, NX)
        columns = pl.ds(s * BLOCK, BLOCK)
        out[:, columns] = pan[:, columns] - ret[away].reshape(square)
        stores.append(pltpu.make_async_copy(out.at[:, columns], out_hbm.at[0, :, columns], out_sems.at[s]))
        stores[-1].start()
    for store in stores:
        store.wait()


def body(factor, pattern, order, targets, panels):
    vm, sem = pltpu.VMEM, pltpu.SemaphoreType.DMA
    f32, bf16 = jnp.float32, jnp.bfloat16
    rows, width = factor.shape[1:]
    tile = (ROWS, BLOCK)
    ret = pl.pallas_call(
        kernel,
        out_shape=jax.ShapeDtypeStruct((4, NR, *tile), f32),
        in_specs=[pl.BlockSpec(memory_space=pl.ANY) for _ in range(3)],
        out_specs=pl.BlockSpec(memory_space=pl.ANY),
        scratch_shapes=[
            pltpu.SMEM((128,), jnp.int32), vm((NX, 8, BLOCK), jnp.int32),
            vm((rows, width), f32), vm((rows, width), f32), vm((rows, width // 2), f32),
            vm((2, rows, width), bf16), vm((2, rows, width), bf16),
            vm((2, rows, width // 2), bf16), vm((2, rows, width // 2), bf16), vm((NX, 8, BLOCK), f32),
            vm((3, NR, *tile), f32), vm((2, NQ, *tile), f32), vm((2, NQ, *tile), f32), vm((3, *tile), f32),
            vm((3, NY, *tile), f32), vm((3, NQ, *tile), f32),
            sem((3,)), sem((3,)), sem((5,)),
            sem((3,)), sem((3,)), sem((3, NY)), sem((3, NY)), sem((2,)), sem((3,)), sem((3,)), sem((2,)),
        ],
        compiler_params=pltpu.CompilerParams(
            collective_id=0, has_side_effects=True, vmem_limit_bytes=60 * 2**20
        ),
        name="fan_in",
    )(order, jnp.transpose(pattern, (1, 2, 0)), factor)
    return pl.pallas_call(
        finish,
        out_shape=jax.ShapeDtypeStruct((1, *panels.shape), f32),
        in_specs=[pl.BlockSpec(memory_space=pl.ANY) for _ in range(3)],
        out_specs=pl.BlockSpec(memory_space=pl.ANY),
        scratch_shapes=[
            pltpu.SMEM((2, 2), jnp.int32),
            vm((4, NR, *tile), f32), vm(panels.shape, f32), vm(panels.shape, f32), sem((6,)), sem((4,)),
        ],
        compiler_params=pltpu.CompilerParams(vmem_limit_bytes=60 * 2**20),
        name="finish",
    )(targets, ret, panels)


def solution(mesh):
    torus = Mesh(mesh.devices.reshape(NY, NZ, NC, NX), (*COL, "x"))
    in_specs = (P(COL, "x", None), P(), P(), P(), P("x", None))
    return jax.shard_map(
        body, mesh=torus, in_specs=in_specs, out_specs=P(COL, "x", None), check_vma=False
    )
```

time: 42.6 us -> 41.4 us (0.972)
  local copies, waits for them, and re-layouts: 1.67 us -> 0 us
    unnamed x1 -> x0, local copies, waits for them, and re-layouts: 1.67 us -> none
    pallas_call x1 -> x2, Pallas kernels: 40.8 us -> 41.1 us  [the longest x1 39.1 us: body(): pl.pallas_call(kernel, out_shape=jax.ShapeDtypeStruct((4, NR, *tile), f32...]
where the time goes in v3:
time: 41.4 us; the launch traced here: 41.1 us
  Pallas kernels  41.1 us (99%)
    pallas_call x1, Pallas kernels, body(): pl.pallas_call(kernel, out_shape=jax.ShapeDtypeStruct((4, NR, *tile), f32...  39.1 us
    pallas_call x1, Pallas kernels, body(): pl.pallas_call(finish, out_shape=jax.ShapeDtypeStruct((1, *panels.shape),...  2.01 us

profile of v3, /device:TPU:1, one launch (start us, length us, event | category | flops | bytes accessed | tf_op | source)
XLA Modules:
  0.0 41.1 jit_solution(7486117019596294714)
XLA Ops:
  0.0 39.1 %fan_in.1.ret_hbm = f32[4,16,8,128]{3,2,1,0:T(8,128)} custom-call(s32[128]{0:T(128)} %order_hbm.1, s32[4,8,128]{2,1,0:T(8,128)} %bitcast.1, f32[1,128,1024]{2,1,0:T(8,128)} %factor_hbm.1), custom_call_target="tpu_custom_call" | custom-call | tf_op jit(solution)/shard_map/fan_in/pallas_call | solution.py:332
  39.1 2.0 %finish.1 = f32[1,128,512]{2,1,0:T(8,128)} custom-call(s32[2,2]{1,0:T(2,128)} %targets_hbm.1, f32[4,16,8,128]{3,2,1,0:T(8,128)} %fan_in.1.ret_hbm, f32[128,512]{1,0:T(8,128)} %panels_hbm.1), custom_call_target="tpu_custom_call" | custom-call | tf_op jit(solution)/shard_map/finish/pallas_call | solution.py:352

commit v4 on v3

--- a/solution.py
+++ b/solution.py
@@ -14,7 +14,8 @@
 BASE = 0 if NR == NQ else NQ - NR // 2
 MESH = pl.DeviceIdType.MESH
 COL = ("y", "z", "core")
-OWN, NEAR, FAR = 0, 1, 2
+OWN, NEAR, FAR, REST = 0, 1, 2, 3
+QUARTER = 256
 FARTHEST_FIRST = (6, 7, 8, 9, 4, 5, 10, 11, 2, 3, 12, 13, 0, 1, 14, 15)
 
 
@@ -34,8 +35,8 @@
 
 def kernel(
     order_hbm, pattern_hbm, factor_hbm, ret,
-    order_ref, pattern_ref, own, near, far, high, low, fhigh, flow, mask,
-    u, f, g, tot, yb, e,
+    order_ref, pattern_ref, own, near, far, high, low, fhigh, flow, rhigh, rlow, mask,
+    u, f, n, g, tot, yb, e,
     heavy_send, heavy_recv, local_sem,
     fwd_send, fwd_recv, y_send, y_recv, ret_send, ret_recv, rt_send, rt_recv,
 ):
@@ -55,11 +56,8 @@
     def scanner(j):
         return lax.rem(j + BASE, NQ)
 
-    def half(row):
-        return pl.ds(pl.multiple_of((row // 2) * 512, 512), 512)
-
-    def other(row):
-        return pl.ds(pl.multiple_of((1 - row // 2) * 512, 512), 512)
+    def quarter(k):
+        return pl.ds(pl.multiple_of(lax.rem(k, NX) * QUARTER, QUARTER), QUARTER)
 
     loads = [
         pltpu.make_async_copy(a, b, local_sem.at[i])
@@ -82,12 +80,8 @@
     for k in range(1, NY):
         greet(at(x, lax.rem(y + k, NY), q))
 
-    @pl.when(scans)
-    def _():
-        for k in range(NZ):
-            greet(at(down, y, k * NC + 1))
-
-    pl.semaphore_wait(barrier, NX + NQ + NY - 3 + c * NR)
+    loads[0].wait()
+    pl.semaphore_wait(barrier, NX + NQ + NY - 3)
 
     def exchange(src, dst, i, row):
         return pltpu.make_async_remote_copy(
@@ -95,12 +89,16 @@
             device_id=at(row, y, q), device_id_type=MESH,
         )
 
-    first = exchange(factor_hbm.at[0, :, half(ahead)], near.at[:, half(ahead)], 0, ahead)
-    second = exchange(factor_hbm.at[0, :, other(ahead)], near.at[:, other(ahead)], 1, ahead)
-    third = exchange(factor_hbm.at[0, :, half(behind)], far, 2, behind)
-    first.start()
-    third.start()
-    second.start()
+    near_parts = [
+        exchange(own.at[:, quarter(ahead + k)], near.at[:, quarter(ahead + k)], i, ahead)
+        for i, k in enumerate((0, 1, 2 + c))
+    ]
+    far_parts = [
+        exchange(own.at[:, quarter(behind + k)], far.at[:, pl.ds(k * QUARTER, QUARTER)], 3 + k, behind)
+        for k in range(2)
+    ]
+    for part in (near_parts[0], far_parts[0], near_parts[1], far_parts[1], near_parts[2]):
+        part.start()
 
     loads[1].wait()
     loads[2].wait()
@@ -145,29 +143,32 @@
         def _():
             wait_slots(buffer, large, sem)
 
-    def forward(b, row):
+    def forward(b, to, row):
         for j in FARTHEST_FIRST:
-            to = scanner(j)
-
-            @pl.when(jnp.logical_or(row != x, to != q))
+            @pl.when(jnp.logical_or(row != x, j != q))
             def _():
-                send(u.at[b, j], f.at[b, q], fwd_send.at[b], fwd_recv.at[b], at(row, y, to))
-
-        @pl.when(jnp.logical_and(scans, row == x))
-        def _():
-            f[b, q] = u[b, slot]
+                send(u.at[b, j], to.at[q], fwd_send.at[b], fwd_recv.at[NEAR if b == REST else b], at(row, y, j))
+
+        @pl.when(row == x)
+        def _():
+            to[q] = u[b, slot]
 
     def scan(b, part):
-        total = part(0)
-        e[b, 0] = total
-        for s in range(1, NQ):
-            total = total + part(s)
-            e[b, s] = total
-        tot[b] = total
+        parts = [part(s) for s in range(NQ)]
+        level = parts
+        while len(level) > 1:
+            level = [level[k] + level[k + 1] for k in range(0, len(level), 2)]
+        tot[b] = level[0]
         for k in range(1, NY):
             @pl.when(k > y)
             def _():
                 send(tot.at[b], yb.at[b, y], y_send.at[b, k], y_recv.at[b, y], at(x, k, q))
+
+        total = parts[0]
+        e[b, 0] = total
+        for s in range(1, NQ):
+            total = total + parts[s]
+            e[b, s] = total
 
     def total_waits(b, earlier):
         for k in range(NY):
@@ -184,26 +185,45 @@
         for s in range(NQ):
             e[b, s] = e[b, s] + before
 
-    loads[0].wait()
     prepare(own, x, 0, 8, put_at(c))
     keep(OWN, product(high[c], low[c], high[c], low[c]))
-    forward(OWN, x)
+    forward(OWN, f, x)
 
     @pl.when(scans)
     def _():
-        wait_slots(f.at[OWN], NQ - 1, fwd_recv.at[OWN])
-        scan(OWN, lambda s: f[OWN, s])
-
-    first.wait_recv()
-    third.wait_recv()
-    for k in range(4):
-        columns = pl.ds(k * BLOCK, BLOCK)
-        block = (x // 2) * 4 + k
-        from_near = near[:, pl.ds(pl.multiple_of(block * BLOCK, BLOCK), BLOCK)]
-        for value, row in ((from_near, behind), (far[:, columns], ahead)):
-            h, l = split(value * mask[row, pl.ds(block, 1), :])
-            fhigh[row // 2, :, columns] = h
-            flow[row // 2, :, columns] = l
+        wait_slots(f, NQ - 1, fwd_recv.at[OWN])
+        scan(OWN, lambda s: f[s])
+
+    def masked(value, row, block):
+        return split(value * mask[row, pl.ds(block, 1), :])
+
+    def prepare_near(k):
+        blocks = []
+        for i in range(2):
+            block = lax.rem(k, NX) * 2 + i
+            columns = pl.ds(pl.multiple_of(block * BLOCK, BLOCK), BLOCK)
+            h, l = masked(near[:, columns], behind, block)
+            high[1 - c, :, columns] = h
+            low[1 - c, :, columns] = l
+            blocks.append((h, l))
+        return blocks
+
+    for k in range(2):
+        near_parts[k].wait_recv()
+        far_parts[k].wait_recv()
+        for i, (h, l) in enumerate(prepare_near(x + k)):
+            columns = pl.ds((2 * k + i) * BLOCK, BLOCK)
+            fhigh[behind // 2, :, columns] = h
+            flow[behind // 2, :, columns] = l
+            h, l = masked(far[:, columns], ahead, lax.rem(x + k, NX) * 2 + i)
+            fhigh[ahead // 2, :, columns] = h
+            flow[ahead // 2, :, columns] = l
+
+            @pl.when(c == k)
+            def _():
+                rhigh[c, :, pl.ds(i * BLOCK, BLOCK)] = h
+                rlow[c, :, pl.ds(i * BLOCK, BLOCK)] = l
+
     keep(FAR, product(fhigh[0], flow[0], fhigh[1], flow[1]))
     for j in FARTHEST_FIRST:
         row = jnp.where(lax.rem(j // NC, 2) == x // 2, x, across)
@@ -216,11 +236,20 @@
     def _():
         g[x // 2, q] = u[FAR, slot]
 
-    prepare(near, behind, (x // 2) * 4, 4, put_at(1 - c))
-    second.wait_recv()
-    prepare(near, behind, (1 - x // 2) * 4, 4, put_at(1 - c))
-    keep(NEAR, product(high[0], low[0], high[1], low[1]))
-    forward(NEAR, lax.rem(x + c, NX))
+    rhigh[1 - c] = high[c, :, quarter(x + c)]
+    rlow[1 - c] = low[c, :, quarter(x + c)]
+    keep(REST, product(rhigh[0], rlow[0], rhigh[1], rlow[1]))
+    forward(REST, n.at[1], lax.rem(x + 1 - c, NX))
+
+    def near_on(k):
+        columns = quarter(k)
+        return product(high[0, :, columns], low[0, :, columns], high[1, :, columns], low[1, :, columns])
+
+    early = near_on(x) + near_on(x + 1)
+    near_parts[2].wait_recv()
+    prepare_near(x + 2 + c)
+    keep(NEAR, early + near_on(x + 2 + c))
+    forward(NEAR, n.at[0], lax.rem(x + c, NX))
 
     @pl.when(scans)
     def _():
@@ -239,8 +268,8 @@
             wait_slots(flat, 2 * NQ - 1, fwd_recv.at[FAR])
             scan(FAR, lambda s: g[0, s] + g[1, s])
 
-        either(c == 0, NQ - 1, NQ, f.at[NEAR], fwd_recv.at[NEAR])
-        scan(NEAR, lambda s: f[NEAR, s])
+        wait_slots(n.reshape(2 * NQ, ROWS, BLOCK), 2 * NQ - 1, fwd_recv.at[NEAR])
+        scan(NEAR, lambda s: n[0, s] + n[1, s])
 
         def far_back(places):
             for p in places:
@@ -273,17 +302,12 @@
         keep_own.wait()
         keep_near.wait()
 
-    either(scans, NR - 1, NR, ret.at[0], ret_recv.at[0])
-    wait_slots(ret.at[2], NR, ret_recv.at[2])
-    either(scans, NR - 1, NR, ret.at[1], ret_recv.at[1])
-    wait_slots(ret.at[3], NR, rt_recv.at[0])
-
-    first.wait_send()
-    second.wait_send()
-    third.wait_send()
+    for part in (*near_parts, *far_parts):
+        part.wait_send()
     wait_slots(u.at[OWN], NR - 1, fwd_send.at[OWN])
     either(joins, NR - 1, NR, u.at[FAR], fwd_send.at[FAR])
-    either(jnp.logical_and(scans, c == 0), NR - 1, NR, u.at[NEAR], fwd_send.at[NEAR])
+    either(c == 0, NR - 1, NR, u.at[NEAR], fwd_send.at[NEAR])
+    either(c == 1, NR - 1, NR, u.at[REST], fwd_send.at[REST])
 
     @pl.when(scans)
     def _():
@@ -299,26 +323,37 @@
             wait_slots(e.at[FAR], NQ, rt_send.at[1])
             wait_slots(e.at[FAR], NQ, rt_send.at[2])
 
+    either(scans, NR - 1, NR, ret.at[0], ret_recv.at[0])
+    wait_slots(ret.at[2], NR, ret_recv.at[2])
+    either(scans, NR - 1, NR, ret.at[1], ret_recv.at[1])
+    wait_slots(ret.at[3], NR, rt_recv.at[0])
+
 
 def finish(targets_hbm, ret_hbm, panels_hbm, out_hbm, targets_ref, ret, pan, out, sems, out_sems):
     x = lax.axis_index("x")
     square = (BLOCK, BLOCK)
     loads = [pltpu.make_async_copy(ret_hbm.at[k], ret.at[k], sems.at[k]) for k in range(4)]
-    loads.append(pltpu.make_async_copy(panels_hbm, pan, sems.at[4]))
-    loads.append(pltpu.make_async_copy(targets_hbm, targets_ref, sems.at[5]))
+    load_pan = pltpu.make_async_copy(panels_hbm, pan, sems.at[4])
+    load_targets = pltpu.make_async_copy(targets_hbm, targets_ref, sems.at[5])
+    load_targets.start()
+    load_pan.start()
     for load in loads:
         load.start()
-    for load in loads:
-        load.wait()
-    ret[3] = ret[3].reshape(square).T.reshape(ret.shape[1:])
-    pair = ret[2].reshape(square)
-    ret[2] = jnp.where(x < 2, pair, pair.T).reshape(ret.shape[1:])
+    load_targets.wait()
+    load_pan.wait()
     stores = []
-    for s in range(4):
-        away = lax.rem(x - targets_ref[s // 2, s % 2] + NX, NX)
-        columns = pl.ds(s * BLOCK, BLOCK)
-        out[:, columns] = pan[:, columns] - ret[away].reshape(square)
-        stores.append(pltpu.make_async_copy(out.at[:, columns], out_hbm.at[0, :, columns], out_sems.at[s]))
+    for k in range(4):
+        loads[k].wait()
+        block = ret[k].reshape(square)
+        if k == 2:
+            block = jnp.where(x < 2, block, block.T)
+        elif k == 3:
+            block = block.T
+        row = lax.rem(x - k + NX, NX)
+        place = sum(jnp.where(targets_ref[s // 2, s % 2] == row, s, 0) for s in range(4))
+        columns = pl.ds(pl.multiple_of(place * BLOCK, BLOCK), BLOCK)
+        out[:, columns] = pan[:, columns] - block
+        stores.append(pltpu.make_async_copy(out.at[:, columns], out_hbm.at[0, :, columns], out_sems.at[k]))
         stores[-1].start()
     for store in stores:
         store.wait()
@@ -338,11 +373,12 @@
             pltpu.SMEM((128,), jnp.int32), vm((NX, 8, BLOCK), jnp.int32),
             vm((rows, width), f32), vm((rows, width), f32), vm((rows, width // 2), f32),
             vm((2, rows, width), bf16), vm((2, rows, width), bf16),
-            vm((2, rows, width // 2), bf16), vm((2, rows, width // 2), bf16), vm((NX, 8, BLOCK), f32),
-            vm((3, NR, *tile), f32), vm((2, NQ, *tile), f32), vm((2, NQ, *tile), f32), vm((3, *tile), f32),
+            vm((2, rows, width // 2), bf16), vm((2, rows, width // 2), bf16),
+            vm((2, rows, QUARTER), bf16), vm((2, rows, QUARTER), bf16), vm((NX, 8, BLOCK), f32),
+            vm((4, NR, *tile), f32), vm((NQ, *tile), f32), vm((2, NQ, *tile), f32), vm((2, NQ, *tile), f32), vm((3, *tile), f32),
             vm((3, NY, *tile), f32), vm((3, NQ, *tile), f32),
-            sem((3,)), sem((3,)), sem((5,)),
-            sem((3,)), sem((3,)), sem((3, NY)), sem((3, NY)), sem((2,)), sem((3,)), sem((3,)), sem((2,)),
+            sem((5,)), sem((5,)), sem((5,)),
+            sem((4,)), sem((3,)), sem((3, NY)), sem((3, NY)), sem((2,)), sem((3,)), sem((3,)), sem((2,)),
         ],
         compiler_params=pltpu.CompilerParams(
             collective_id=0, has_side_effects=True, vmem_limit_bytes=60 * 2**20

time: 41.4 us -> 41.4 us (level)
  the two profiles are of different devices: /device:TPU:1 before, /device:TPU:59 now
where the time goes in v4:
time: 41.4 us; the launch traced here: 41.2 us
  Pallas kernels  41.2 us (100%)
    pallas_call x1, Pallas kernels, body(): pl.pallas_call(kernel, out_shape=jax.ShapeDtypeStruct((4, NR, *tile), f32...  39.3 us
    pallas_call x1, Pallas kernels, body(): pl.pallas_call(finish, out_shape=jax.ShapeDtypeStruct((1, *panels.shape),...  1.91 us

profile of v4, /device:TPU:59, one launch (start us, length us, event | category | flops | bytes accessed | tf_op | source)
XLA Modules:
  0.0 41.2 jit_solution(8370436161890034946)
XLA Ops:
  0.0 39.3 %fan_in.1.ret_hbm = f32[4,16,8,128]{3,2,1,0:T(8,128)} custom-call(s32[128]{0:T(128)} %order_hbm.1, s32[4,8,128]{2,1,0:T(8,128)} %bitcast.1, f32[1,128,1024]{2,1,0:T(8,128)} %factor_hbm.1), custom_call_target="tpu_custom_call" | custom-call | tf_op jit(solution)/shard_map/fan_in/pallas_call | solution.py:367
  39.3 1.9 %finish.1 = f32[1,128,512]{2,1,0:T(8,128)} custom-call(s32[2,2]{1,0:T(2,128)} %targets_hbm.1, f32[4,16,8,128]{3,2,1,0:T(8,128)} %fan_in.1.ret_hbm, f32[128,512]{1,0:T(8,128)} %panels_hbm.1), custom_call_target="tpu_custom_call" | custom-call | tf_op jit(solution)/shard_map/finish/pallas_call | solution.py:388

commit v5 on v3

--- a/solution.py
+++ b/solution.py
@@ -79,15 +79,14 @@
         greet(at(lax.rem(x + k, NX), y, q))
     for k in range(1, NQ):
         greet(at(x, y, lax.rem(q + k, NQ)))
-    for k in range(1, NY):
-        greet(at(x, lax.rem(y + k, NY), q))
-
-    @pl.when(scans)
-    def _():
-        for k in range(NZ):
-            greet(at(down, y, k * NC + 1))
-
-    pl.semaphore_wait(barrier, NX + NQ + NY - 3 + c * NR)
+    for k in range(NY - 1):
+        @pl.when(k < y)
+        def _():
+            greet(at(x, k, q))
+
+
+    loads[0].wait()
+    pl.semaphore_wait(barrier, NX + NQ + NY - 3 - y)
 
     def exchange(src, dst, i, row):
         return pltpu.make_async_remote_copy(
@@ -95,12 +94,16 @@
             device_id=at(row, y, q), device_id_type=MESH,
         )
 
-    first = exchange(factor_hbm.at[0, :, half(ahead)], near.at[:, half(ahead)], 0, ahead)
-    second = exchange(factor_hbm.at[0, :, other(ahead)], near.at[:, other(ahead)], 1, ahead)
-    third = exchange(factor_hbm.at[0, :, half(behind)], far, 2, behind)
-    first.start()
+    near_parts = [
+        exchange(own.at[rows, columns(ahead)], near.at[rows, columns(ahead)], i, ahead)
+        for i, (rows, columns) in enumerate((r, k) for k in (half, other) for r in (pl.ds(0, 64), pl.ds(64, 64)))
+    ]
+    third = exchange(own.at[:, half(behind)], far, 4, behind)
+    near_parts[0].start()
+    near_parts[1].start()
     third.start()
-    second.start()
+    near_parts[2].start()
+    near_parts[3].start()
 
     loads[1].wait()
     loads[2].wait()
@@ -158,16 +161,21 @@
             f[b, q] = u[b, slot]
 
     def scan(b, part):
-        total = part(0)
-        e[b, 0] = total
-        for s in range(1, NQ):
-            total = total + part(s)
-            e[b, s] = total
-        tot[b] = total
+        parts = [part(s) for s in range(NQ)]
+        level = parts
+        while len(level) > 1:
+            level = [level[k] + level[k + 1] for k in range(0, len(level), 2)]
+        tot[b] = level[0]
         for k in range(1, NY):
             @pl.when(k > y)
             def _():
                 send(tot.at[b], yb.at[b, y], y_send.at[b, k], y_recv.at[b, y], at(x, k, q))
+
+        total = parts[0]
+        e[b, 0] = total
+        for s in range(1, NQ):
+            total = total + parts[s]
+            e[b, s] = total
 
     def total_waits(b, earlier):
         for k in range(NY):
@@ -184,7 +192,6 @@
         for s in range(NQ):
             e[b, s] = e[b, s] + before
 
-    loads[0].wait()
     prepare(own, x, 0, 8, put_at(c))
     keep(OWN, product(high[c], low[c], high[c], low[c]))
     forward(OWN, x)
@@ -194,7 +201,8 @@
         wait_slots(f.at[OWN], NQ - 1, fwd_recv.at[OWN])
         scan(OWN, lambda s: f[OWN, s])
 
-    first.wait_recv()
+    near_parts[0].wait_recv()
+    near_parts[1].wait_recv()
     third.wait_recv()
     for k in range(4):
         columns = pl.ds(k * BLOCK, BLOCK)
@@ -217,7 +225,8 @@
         g[x // 2, q] = u[FAR, slot]
 
     prepare(near, behind, (x // 2) * 4, 4, put_at(1 - c))
-    second.wait_recv()
+    near_parts[2].wait_recv()
+    near_parts[3].wait_recv()
     prepare(near, behind, (1 - x // 2) * 4, 4, put_at(1 - c))
     keep(NEAR, product(high[0], low[0], high[1], low[1]))
     forward(NEAR, lax.rem(x + c, NX))
@@ -273,13 +282,10 @@
         keep_own.wait()
         keep_near.wait()
 
-    either(scans, NR - 1, NR, ret.at[0], ret_recv.at[0])
-    wait_slots(ret.at[2], NR, ret_recv.at[2])
-    either(scans, NR - 1, NR, ret.at[1], ret_recv.at[1])
-    wait_slots(ret.at[3], NR, rt_recv.at[0])
-
-    first.wait_send()
-    second.wait_send()
+    near_parts[0].wait_send()
+    near_parts[1].wait_send()
+    near_parts[2].wait_send()
+    near_parts[3].wait_send()
     third.wait_send()
     wait_slots(u.at[OWN], NR - 1, fwd_send.at[OWN])
     either(joins, NR - 1, NR, u.at[FAR], fwd_send.at[FAR])
@@ -299,26 +305,37 @@
             wait_slots(e.at[FAR], NQ, rt_send.at[1])
             wait_slots(e.at[FAR], NQ, rt_send.at[2])
 
+    either(scans, NR - 1, NR, ret.at[0], ret_recv.at[0])
+    wait_slots(ret.at[2], NR, ret_recv.at[2])
+    either(scans, NR - 1, NR, ret.at[1], ret_recv.at[1])
+    wait_slots(ret.at[3], NR, rt_recv.at[0])
+
 
 def finish(targets_hbm, ret_hbm, panels_hbm, out_hbm, targets_ref, ret, pan, out, sems, out_sems):
     x = lax.axis_index("x")
     square = (BLOCK, BLOCK)
     loads = [pltpu.make_async_copy(ret_hbm.at[k], ret.at[k], sems.at[k]) for k in range(4)]
-    loads.append(pltpu.make_async_copy(panels_hbm, pan, sems.at[4]))
-    loads.append(pltpu.make_async_copy(targets_hbm, targets_ref, sems.at[5]))
+    load_pan = pltpu.make_async_copy(panels_hbm, pan, sems.at[4])
+    load_targets = pltpu.make_async_copy(targets_hbm, targets_ref, sems.at[5])
+    load_targets.start()
+    load_pan.start()
     for load in loads:
         load.start()
-    for load in loads:
-        load.wait()
-    ret[3] = ret[3].reshape(square).T.reshape(ret.shape[1:])
-    pair = ret[2].reshape(square)
-    ret[2] = jnp.where(x < 2, pair, pair.T).reshape(ret.shape[1:])
+    load_targets.wait()
+    load_pan.wait()
     stores = []
-    for s in range(4):
-        away = lax.rem(x - targets_ref[s // 2, s % 2] + NX, NX)
-        columns = pl.ds(s * BLOCK, BLOCK)
-        out[:, columns] = pan[:, columns] - ret[away].reshape(square)
-        stores.append(pltpu.make_async_copy(out.at[:, columns], out_hbm.at[0, :, columns], out_sems.at[s]))
+    for k in range(4):
+        loads[k].wait()
+        block = ret[k].reshape(square)
+        if k == 2:
+            block = jnp.where(x < 2, block, block.T)
+        elif k == 3:
+            block = block.T
+        row = lax.rem(x - k + NX, NX)
+        place = sum(jnp.where(targets_ref[s // 2, s % 2] == row, s, 0) for s in range(4))
+        columns = pl.ds(pl.multiple_of(place * BLOCK, BLOCK), BLOCK)
+        out[:, columns] = pan[:, columns] - block
+        stores.append(pltpu.make_async_copy(out.at[:, columns], out_hbm.at[0, :, columns], out_sems.at[k]))
         stores[-1].start()
     for store in stores:
         store.wait()
@@ -341,7 +358,7 @@
             vm((2, rows, width // 2), bf16), vm((2, rows, width // 2), bf16), vm((NX, 8, BLOCK), f32),
             vm((3, NR, *tile), f32), vm((2, NQ, *tile), f32), vm((2, NQ, *tile), f32), vm((3, *tile), f32),
             vm((3, NY, *tile), f32), vm((3, NQ, *tile), f32),
-            sem((3,)), sem((3,)), sem((5,)),
+            sem((5,)), sem((5,)), sem((5,)),
             sem((3,)), sem((3,)), sem((3, NY)), sem((3, NY)), sem((2,)), sem((3,)), sem((3,)), sem((2,)),
         ],
         compiler_params=pltpu.CompilerParams(

time: 41.4 us -> 41.2 us (level)
  Pallas kernels: 41.1 us -> 40.5 us
    pallas_call x1, Pallas kernels: 39.1 us -> 38.6 us  [body(): pl.pallas_call(kernel, out_shape=jax.ShapeDtypeStruct((4, NR, *tile), f32...]
where the time goes in v5:
time: 41.2 us; the launch traced here: 40.5 us
  Pallas kernels  40.5 us (98%)
    pallas_call x1, Pallas kernels, body(): pl.pallas_call(kernel, out_shape=jax.ShapeDtypeStruct((4, NR, *tile), f32...  38.6 us
    pallas_call x1, Pallas kernels, body(): pl.pallas_call(finish, out_shape=jax.ShapeDtypeStruct((1, *panels.shape),...  1.91 us

profile of v5, /device:TPU:1, one launch (start us, length us, event | category | flops | bytes accessed | tf_op | source)
XLA Modules:
  0.0 40.5 jit_solution(10306403420170308836)
XLA Ops:
  0.0 38.6 %fan_in.1.ret_hbm = f32[4,16,8,128]{3,2,1,0:T(8,128)} custom-call(s32[128]{0:T(128)} %order_hbm.1, s32[4,8,128]{2,1,0:T(8,128)} %bitcast.1, f32[1,128,1024]{2,1,0:T(8,128)} %factor_hbm.1), custom_call_target="tpu_custom_call" | custom-call | tf_op jit(solution)/shard_map/fan_in/pallas_call | solution.py:349
  38.6 1.9 %finish.1 = f32[1,128,512]{2,1,0:T(8,128)} custom-call(s32[2,2]{1,0:T(2,128)} %targets_hbm.1, f32[4,16,8,128]{3,2,1,0:T(8,128)} %fan_in.1.ret_hbm, f32[128,512]{1,0:T(8,128)} %panels_hbm.1), custom_call_target="tpu_custom_call" | custom-call | tf_op jit(solution)/shard_map/finish/pallas_call | solution.py:369
